TPU v7x, 32 devices: a whole 2x2x4 slice. The times are simulated.
32 devices in a mesh: groups: 2 (over x), dp: 8 (over z, y), expert: 2 (over core).
Axes of the slice: x: 2, y: 2, z: 4, core: 2. Of those that a mesh axis runs over, the one named last changes fastest.
Arguments:
- tokens: bfloat16 [4096, 6144], P(('groups', 'dp', 'expert')), parts along dimension 0, may hold values from -6 to 6
- out_grads: bfloat16 [4096, 2, 6144], P(('groups', 'dp', 'expert')), parts along dimension 0, may hold values from -6 to 6
- expert_ids: int32 [4096, 2], P(('groups', 'dp', 'expert')), parts along dimension 0, may hold values from 0 to 3, all different within a row; in each aligned block of 128 rows (0 to 127, 128 to 255, ...) at most 96 rows name the same one
Outputs:
- act_factor: float32 [64, 4, 6144], P(('groups', 'dp'), 'expert'), parts along dimension 0
- grad_factor: float32 [64, 4, 6144], P(('groups', 'dp'), 'expert'), parts along dimension 0
There are 2 independent parts, one for each index of `groups`. A program takes and returns all parts, laid end to end along the dimension named above; each array names one. Nothing has to cross between parts.
Inputs may be any that keep to these rules, and one draw needn't show every extreme that they name: `expert_ids`: each row names 2 different experts. In the 128 rows of one device no expert is named by more than 96 rows, a bound that some block reaches of them.
All inputs are finite; a program needn't handle non-finite values.
Results may differ from a plain program's by a relative error of at most 0.0003.
Values may be sent and summed in bfloat16 or wider, within the bound.
A program may use at most 128 MiB of HBM per device.

v0:
```python
import jax
import jax.numpy as jnp
from jax import lax
from jax.sharding import PartitionSpec as P

EXP_DEV = 2
ROWS_DEV = 4
CAP = 96


def build_buffer(rows, target, slots):
    empty = jnp.zeros((slots, rows.shape[1]), rows.dtype)
    return empty.at[target].set(rows)


def on_device(tokens, out_grads, expert_ids):
    tok_rows, features = tokens.shape
    top_count = expert_ids.shape[1]
    dp_count = lax.axis_size("dp")
    core_count = lax.axis_size("expert")
    expert_count = EXP_DEV * core_count
    token_total = tok_rows * dp_count * core_count
    slab_rows = ROWS_DEV * dp_count
    flat_ids = expert_ids.reshape(-1)
    onehot = (flat_ids[:, None] == jnp.arange(expert_count, dtype=jnp.int32)[None, :]).astype(
        jnp.int32
    )
    before = jnp.cumsum(onehot, axis=0) - onehot
    slot_index = jnp.sum(before * onehot, axis=1)
    target = flat_ids * CAP + slot_index
    input_rows = jnp.broadcast_to(tokens[:, None, :], (tok_rows, top_count, features)).reshape(
        -1, features
    )
    grad_rows = out_grads.reshape(-1, features)
    input_send = build_buffer(input_rows, target, expert_count * CAP).reshape(
        expert_count, CAP, features
    )
    grad_send = build_buffer(grad_rows, target, expert_count * CAP).reshape(
        expert_count, CAP, features
    )
    input_recv, grad_recv = (
        lax.all_to_all(input_send, "expert", split_axis=0, concat_axis=1, tiled=True),
        lax.all_to_all(grad_send, "expert", split_axis=0, concat_axis=1, tiled=True),
    )
    act_term = jnp.einsum(
        "nsr,nsc->rnc", input_recv[:, :, :slab_rows], input_recv, preferred_element_type=jnp.float32
    )
    grad_term = jnp.einsum(
        "nsr,nsc->rnc", grad_recv[:, :, :slab_rows], grad_recv, preferred_element_type=jnp.float32
    )
    act_sum, grad_sum = (
        lax.psum_scatter(act_term, "dp", scatter_dimension=0, tiled=True),
        lax.psum_scatter(grad_term, "dp", scatter_dimension=0, tiled=True),
    )
    return (act_sum / token_total, grad_sum / token_total)


def solution(mesh):
    placed = (
        P(("groups", "dp", "expert"), None),
        P(("groups", "dp", "expert"), None, None),
        P(("groups", "dp", "expert"), None),
    )
    return jax.shard_map(
        on_device,
        mesh=mesh,
        in_specs=placed,
        out_specs=(P(("groups", "dp"), "expert", None), P(("groups", "dp"), "expert", None)),
        check_vma=False,
    )
```

profile of v0, /device:TPU:0, one launch (start us, length us, event | category | flops | bytes accessed | tf_op | source)
XLA Modules:
  0.0 201.4 jit_solution(4725758311721798611)
XLA Ops:
  7.2 0.8 copy.23
  8.0 0.1 eq.29
  8.1 0.1 eq.25
  8.2 0.7 broadcast_multiply_fusion
  8.9 1.2 reduce-window.6
  10.1 0.1 slice.16
  10.2 0.1 copy.25
  10.4 0.1 copy.26
  10.4 0.1 add_bitcast_fusion
  10.5 0.1 copy.22
  10.6 0.1 mul.21
  10.8 3.3 %broadcast_in_dim.2 = bf16[128,2,6144]{2,1,0:T(2,128)(2,1)S(1)} broadcast(bf16[128,6144]{1,0:T(8,128)(2,1)} %param.3), dimensions={0,2} | broadcast | bytes 4718592 | tf_op jit(solution)/shard_map/broadcast_in_dim | solution.py:31
  14.1 2.7 %reshape.72 = bf16[256,6144]{1,0:T(8,128)(2,1)} reshape(bf16[128,2,6144]{2,1,0:T(2,128)(2,1)S(1)} %broadcast_in_dim.2) | data formatting | bytes 6291456 | tf_op jit(solution)/shard_map/reshape | solution.py:31
  16.8 8.9 %scatter_custom_fusion = bf16[384,6144]{1,0:T(8,128)(2,1)} fusion(s32[256]{0:T(256)S(1)} %bitcast.44, bf16[256,6144]{1,0:T(8,128)(2,1)} %reshape.72, bf16[]{:T(256)} %constant.5.clone.1), kind=kCustom, calls=%fused_computation.6 | custom fusion | bytes 4719104 | tf_op jit(solution)/shard_map/scatter | solution.py:13
  25.7 0.0 copy-start
  25.7 6.2 %all-to-all-start = ((bf16[4,96,6144]{2,1,0:T(8,128)(2,1)}), bf16[4,96,6144]{2,1,0:T(8,128)(2,1)}, u32[]{:S(2)}, u32[]{:S(2)}) async-start(bf16[4,96,6144]{2,1,0:T(8,128)(2,1)} %bitcast.41), calls=%async_computation | async-start | bytes 9437184 | tf_op jit(solution)/shard_map/all_to_all | solution.py:42
  32.0 0.0 copy-done
  32.0 2.7 %reshape.80 = bf16[256,6144]{1,0:T(8,128)(2,1)} reshape(bf16[128,2,6144]{2,1,0:T(2,128)(2,1)S(1)} %copy-done) | data formatting | bytes 6291456 | tf_op jit(solution)/shard_map/reshape | solution.py:34
  34.7 9.0 %scatter_custom_fusion.1 = bf16[384,6144]{1,0:T(8,128)(2,1)} fusion(s32[256]{0:T(256)S(1)} %bitcast.45, bf16[256,6144]{1,0:T(8,128)(2,1)} %reshape.80, bf16[]{:T(256)} %constant.5.clone.1), kind=kCustom, calls=%fused_computation.4 | custom fusion | bytes 4719104 | tf_op jit(solution)/shard_map/scatter | solution.py:13
  43.7 0.0 all-to-all-done
  43.7 5.8 %all-to-all-start.1 = ((bf16[4,96,6144]{2,1,0:T(8,128)(2,1)}), bf16[4,96,6144]{2,1,0:T(8,128)(2,1)}, u32[]{:S(2)}, u32[]{:S(2)}) async-start(bf16[4,96,6144]{2,1,0:T(8,128)(2,1)} %bitcast.40), calls=%async_computation.1 | async-start | bytes 9437184 | tf_op jit(solution)/shard_map/all_to_all | solution.py:43
  49.5 0.0 all-reduce.5.cloned.1.call-start
  49.5 2.6 %copy.27 = bf16[2,2,96,6144]{3,2,1,0:T(8,128)(2,1)S(1)} copy(bf16[2,2,96,6144]{3,2,0,1:T(8,128)(2,1)} %bitcast.6) | data formatting | bytes 9437184 | tf_op jit(solution)/shard_map/all_to_all | solution.py:42
  52.2 2.2 %convolution_bitcast_fusion.1 = f32[32,2,6144]{2,0,1:T(8,128)} fusion(bf16[2,192,6144]{2,1,0:T(8,128)(2,1)S(1)} %bitcast.38), kind=kOutput, calls=%fused_computation.3 | convolution fusion | flops 150994944 | bytes 6389760 | tf_op jit(solution)/shard_map/nsr,nsc->rnc/dot_general | solution.py:45
  54.4 0.0 all-to-all-done.1
  54.4 2.6 %copy.29 = bf16[2,2,96,6144]{3,2,1,0:T(8,128)(2,1)S(1)} copy(bf16[2,2,96,6144]{3,2,0,1:T(8,128)(2,1)} %bitcast.11) | data formatting | bytes 9437184 | tf_op jit(solution)/shard_map/all_to_all | solution.py:43
  57.0 0.0 copy-start.1
  57.0 2.2 %convolution_bitcast_fusion = f32[32,2,6144]{2,0,1:T(8,128)} fusion(bf16[2,192,6144]{2,1,0:T(8,128)(2,1)S(1)} %bitcast.39), kind=kOutput, calls=%fused_computation.2 | convolution fusion | flops 150994944 | bytes 6389760 | tf_op jit(solution)/shard_map/nsr,nsc->rnc/dot_general | solution.py:48
  59.2 0.0 all-reduce.5.cloned.1.call-update
  59.3 0.0 copy-done.1
  59.3 0.6 dynamic-slice
  60.5 131.1 %all-reduce.5.cloned.1.call-done = (f32[32,2,6144]{2,0,1:T(8,128)}, f32[32,2,6144]{2,0,1:T(8,128)}) async-done(((f32[32,2,6144]{2,0,1:T(8,128)}, f32[32,2,6144]{2,0,1:T(8,128)}), (f32[32,2,6144]{2,0,1:T(8,128)}, f32[32,2,6144]{2,0,1:T(8,128)})) %all-reduce.5.cloned.1.call-update) | async-done | bytes 3145744
  191.7 1.2 dynamic-slice_multiply_fusion
  192.9 0.8 copy.31
  193.7 0.8 copy.32
  (5 shorter events, 0.1 us)
Async XLA Ops:
  25.7 6.2 %copy-start = (bf16[128,2,6144]{2,1,0:T(2,128)(2,1)S(1)}, bf16[128,2,6144]{2,1,0:T(2,128)(2,1)}, u32[]{:S(2)}) copy-start(bf16[128,2,6144]{2,1,0:T(2,128)(2,1)} %param.4) | copy-start | bytes 9437188
  25.7 17.9 %all-to-all-start = ((bf16[4,96,6144]{2,1,0:T(8,128)(2,1)}), bf16[4,96,6144]{2,1,0:T(8,128)(2,1)}, u32[]{:S(2)}, u32[]{:S(2)}) async-start(bf16[4,96,6144]{2,1,0:T(8,128)(2,1)} %bitcast.41), calls=%async_computation | async-start | bytes 9437184 | tf_op jit(solution)/shard_map/all_to_all | solution.py:42
  43.7 10.7 %all-to-all-start.1 = ((bf16[4,96,6144]{2,1,0:T(8,128)(2,1)}), bf16[4,96,6144]{2,1,0:T(8,128)(2,1)}, u32[]{:S(2)}, u32[]{:S(2)}) async-start(bf16[4,96,6144]{2,1,0:T(8,128)(2,1)} %bitcast.40), calls=%async_computation.1 | async-start | bytes 9437184 | tf_op jit(solution)/shard_map/all_to_all | solution.py:43
  49.5 142.2 %all-reduce.5.cloned.1.call-start = ((), (), s32[]{:S(2)}) async-start(), calls=%async_computation.2 | async-start | bytes 6291456
  57.0 2.3 %copy-start.1 = (u32[32]{0:T(128)S(1)}, u32[32]{0:T(128)}, u32[]{:S(2)}) copy-start(u32[32]{0:T(128)} %constant.19) | copy-start | bytes 388
Sparse Core Ops, SparseCore 0:
  59.4 132.2 all-reduce.4
where the time goes:
time: 202 us; the launch traced here: 201 us
  waiting for transfers between devices  131 us (65%)
  local copies, waits for them, and re-layouts  35.8 us (18%)
  between operations  14.8 us (7%)
  starting transfers between devices  12.1 us (6%)
  matrix products  4.41 us (2%)
  other arithmetic  3.24 us (2%)
    unnamed x2, waiting for transfers between devices  131 us
    scatter x2, local copies, waits for them, and re-layouts, build_buffer(): return empty.at[target].set(rows)  17.9 us
    all_to_all x1, starting transfers between devices, on_device(): lax.all_to_all(input_send, 'expert', split_axis=0, concat_axis=1, tiled=T...  6.21 us
    all_to_all x1, starting transfers between devices, on_device(): lax.all_to_all(grad_send, 'expert', split_axis=0, concat_axis=1, tiled=True)  5.8 us
  transfers between devices with their start and end apart: 3, of which 1 were waited for; matrix products, arithmetic and copies ran while one was open for 8% of the time, Pallas kernels for 0%

commit v1 on v0

v1 whole, which is shorter than its diff:
```python
import functools

import jax
import jax.numpy as jnp
from jax import lax
from jax.experimental import pallas as pl
from jax.experimental.pallas import tpu as pltpu
from jax.sharding import PartitionSpec as P

EXP_DEV = 2
ROWS_DEV = 4
BLK = EXP_DEV * ROWS_DEV
PAIR = 2 * BLK
LANES = 128
WIDTH = 768
STEPS = 8.0
FULL = 32760.0
TINY = 1e-37
LAG_Y, LAG_Z, LAG_OUT = 1, 3, 4


def encode(tiles, dst):
    top = functools.reduce(jnp.maximum, [jnp.abs(t) for t in tiles])
    step = jnp.ceil(jnp.log2(jnp.maximum(top, TINY)) * STEPS)
    scale = jnp.exp2(step * (-1.0 / STEPS)) * FULL
    for j, t in enumerate(tiles):
        dst(j, jnp.round(t * scale).astype(jnp.int32).astype(jnp.int16))
    dst(len(tiles), step.astype(jnp.int32).astype(jnp.int16))


def widen(x):
    return x.astype(jnp.int32).astype(jnp.float32)


def unit_of(codes):
    return jnp.exp2(widen(codes) * (1.0 / STEPS)) * (1.0 / FULL)


def kernel(
    n, width, total,
    ids_ref, tok_ref, grad_ref, act_ref, gout_ref,
    x_buf, g_buf, part, r0, s1, r1, s2, r2,
    in_sem, s0_sem, r0_sem, s1_sem, r1_sem, s2_sem, r2_sem,
):
    tok_rows, features = tok_ref.shape
    items = features // width
    tiles = width // LANES
    nz = n // 2
    half = n * PAIR
    quarter = half // 2
    core = lax.axis_index("expert")
    d = lax.axis_index("dp")
    z, y = d // 2, lax.rem(d, 2)

    flat = grad_ref.reshape(2 * tok_rows, features)
    loads = []
    for i in range(items):
        cols = pl.ds(i * width, width)
        pair = (
            pltpu.make_async_copy(tok_ref.at[:, cols], x_buf.at[i], in_sem.at[0, i]),
            pltpu.make_async_copy(flat.at[:, cols], g_buf.at[i], in_sem.at[1, i]),
        )
        for c in pair:
            c.start()
        loads.append(pair)

    sibling = {"expert": 1 - core}
    across = {"dp": z * 2 + 1 - y}
    peers = [{"dp": lax.rem(z + 1 + j, nz) * 2 + y} for j in range(nz - 1)]
    barrier = pltpu.get_barrier_semaphore()
    for dev in [sibling, across] + peers:
        pl.semaphore_signal(barrier, inc=1, device_id=dev, device_id_type=pl.DeviceIdType.MESH)

    m_rows = 2 * n * BLK
    slab = -(-ROWS_DEV * n // LANES) * LANES

    def row_of(m):
        zd = z + 1 + (m & (n * BLK // 2 - 1)) // BLK
        zd = jnp.where(zd >= nz, zd - nz, zd)
        yd = (y + 1 + (m & (n * BLK - 1)) // (n * BLK // 2)) & 1
        return ROWS_DEV * (2 * zd + yd) + (m & (BLK - 1)) // EXP_DEV

    def expert_of(m):
        return EXP_DEV * ((core + 1 + m // (n * BLK)) & 1) + (m & (EXP_DEV - 1))

    pick = (
        row_of(lax.broadcasted_iota(jnp.int32, (m_rows, slab), 0))
        == lax.broadcasted_iota(jnp.int32, (m_rows, slab), 1)
    ).astype(jnp.float32).astype(jnp.bfloat16)
    ids = ids_ref[...]
    spread = (
        lax.broadcasted_iota(jnp.int32, (tok_rows, 2 * tok_rows), 1) // 2
        == lax.broadcasted_iota(jnp.int32, (tok_rows, 2 * tok_rows), 0)
    ).astype(jnp.float32).astype(jnp.bfloat16)
    ids_f = ids.astype(jnp.float32)
    both = jnp.dot(ids_f.astype(jnp.bfloat16), spread, preferred_element_type=jnp.float32)
    odd = (lax.broadcasted_iota(jnp.int32, (1, 2 * tok_rows), 1) & 1) == 1
    ids_flat = jnp.where(odd, both[1:2, :], both[0:1, :])
    e_tok = expert_of(lax.broadcasted_iota(jnp.int32, (m_rows, tok_rows), 0)).astype(jnp.float32)
    e_pair = expert_of(lax.broadcasted_iota(jnp.int32, (m_rows, 2 * tok_rows), 0)).astype(
        jnp.float32
    )
    nt = (((1,), (1,)), ((), ()))

    for c in loads[0]:
        c.wait()
    left_x = lax.dot_general(pick, x_buf[0, :, :slab], nt, preferred_element_type=jnp.float32)
    left_g = lax.dot_general(pick, g_buf[0, :, :slab], nt, preferred_element_type=jnp.float32)
    hit_x = (e_tok == ids_f[0:1, :]) | (e_tok == ids_f[1:2, :])
    left_x = jnp.where(hit_x, left_x, 0.0).astype(jnp.bfloat16)
    left_g = jnp.where(e_pair == ids_flat, left_g, 0.0).astype(jnp.bfloat16)

    pl.semaphore_wait(barrier, nz + 1)

    def send(src, dst, s_sem, r_sem, dev):
        return pltpu.make_async_remote_copy(
            src_ref=src, dst_ref=dst, send_sem=s_sem, recv_sem=r_sem,
            device_id=dev, device_id_type=pl.DeviceIdType.MESH,
        )

    core_copy = [
        send(part.at[i, pl.ds(0, half)], r0.at[i], s0_sem.at[i], r0_sem.at[i], sibling)
        for i in range(items)
    ]
    y_copy = [
        send(s1.at[i], r1.at[i], s1_sem.at[i], r1_sem.at[i], across) for i in range(items)
    ]
    z_copy = [
        [
            send(s2.at[i, j], r2.at[i, j], s2_sem.at[i, j], r2_sem.at[i, j], peers[j])
            for j in range(nz - 1)
        ]
        for i in range(items)
    ]

    def local_terms(i):
        if i:
            for c in loads[i]:
                c.wait()
        for a, (left, buf) in enumerate(((left_x, x_buf), (left_g, g_buf))):
            term = jnp.dot(left, buf[i], preferred_element_type=jnp.float32)
            for b in range(m_rows // BLK):
                part[i, b * PAIR + a * BLK : b * PAIR + (a + 1) * BLK, :] = term[
                    b * BLK : (b + 1) * BLK
                ]
        core_copy[i].start()

    def lane(j):
        return slice(j * LANES, (j + 1) * LANES)

    def chip_terms(i):
        core_copy[i].wait_recv()
        for b in range(quarter // PAIR):
            rows = slice(b * PAIR, (b + 1) * PAIR)
            own = slice(half + b * PAIR, half + (b + 1) * PAIR)
            sums = [part[i, own, lane(j)] + r0[i, rows, lane(j)] for j in range(tiles)]

            def put(j, v):
                s1[i, rows, lane(j)] = v

            encode(sums, put)
        y_copy[i].start()

    def pair_terms(i):
        y_copy[i].wait_recv()
        for b in range(nz):
            rows = slice(b * PAIR, (b + 1) * PAIR)
            near = slice(quarter + b * PAIR, quarter + (b + 1) * PAIR)
            own = slice(half + quarter + b * PAIR, half + quarter + (b + 1) * PAIR)
            unit = unit_of(r1[i, rows, lane(tiles)])
            sums = [
                part[i, own, lane(j)]
                + r0[i, near, lane(j)]
                + widen(r1[i, rows, lane(j)]) * unit
                for j in range(tiles)
            ]
            if b < nz - 1:

                def put(j, v):
                    s2[i, b, :, lane(j)] = v

                encode(sums, put)
                z_copy[i][b].start()
            else:
                for j in range(tiles):
                    part[i, own, lane(j)] = sums[j]

    def outputs(i):
        for c in z_copy[i]:
            c.wait_recv()
        last = slice(2 * half - PAIR, 2 * half)
        units = [unit_of(r2[i, b, :, lane(tiles)]) for b in range(nz - 1)]
        for j in range(tiles):
            acc = part[i, last, lane(j)]
            for b in range(nz - 1):
                acc = acc + widen(r2[i, b, :, lane(j)]) * units[b]
            acc = acc * (1.0 / total)
            cols = slice(i * width + j * LANES, i * width + (j + 1) * LANES)
            act_ref[:, cols] = acc[:BLK]
            gout_ref[:, cols] = acc[BLK:]

    for t in range(items + LAG_OUT):
        if t < items:
            local_terms(t)
        if 0 <= t - LAG_Y < items:
            chip_terms(t - LAG_Y)
        if 0 <= t - LAG_Z < items:
            pair_terms(t - LAG_Z)
        if 0 <= t - LAG_OUT < items:
            outputs(t - LAG_OUT)

    for i in range(items):
        core_copy[i].wait_send()
        y_copy[i].wait_send()
        for c in z_copy[i]:
            c.wait_send()


def on_device(n, tokens, out_grads, expert_ids):
    tok_rows, features = tokens.shape
    width = WIDTH if features % WIDTH == 0 else LANES
    items = features // width
    nz = n // 2
    half = n * PAIR
    coded = width + LANES
    total = tok_rows * n * 2
    vmem = pl.BlockSpec(memory_space=pltpu.VMEM)
    hbm = pl.BlockSpec(memory_space=pl.ANY)
    out = jax.ShapeDtypeStruct((BLK, features), jnp.float32)
    dma = pltpu.SemaphoreType.DMA
    flops = 2 * 3 * tok_rows * 2 * n * BLK * features
    act, grad = pl.pallas_call(
        functools.partial(kernel, n, width, total),
        out_shape=(out, out),
        in_specs=[vmem, hbm, hbm],
        out_specs=(vmem, vmem),
        scratch_shapes=[
            pltpu.VMEM((items, tok_rows, width), jnp.bfloat16),
            pltpu.VMEM((items, 2 * tok_rows, width), jnp.bfloat16),
            pltpu.VMEM((items, 2 * half, width), jnp.float32),
            pltpu.VMEM((items, half, width), jnp.float32),
            pltpu.VMEM((items, half // 2, coded), jnp.int16),
            pltpu.VMEM((items, half // 2, coded), jnp.int16),
            pltpu.VMEM((items, nz - 1, PAIR, coded), jnp.int16),
            pltpu.VMEM((items, nz - 1, PAIR, coded), jnp.int16),
            dma((2, items)),
            dma((items,)),
            dma((items,)),
            dma((items,)),
            dma((items,)),
            dma((items, nz - 1)),
            dma((items, nz - 1)),
        ],
        compiler_params=pltpu.CompilerParams(
            collective_id=0, has_side_effects=True, vmem_limit_bytes=61 * 1024 * 1024
        ),
        cost_estimate=pl.CostEstimate(
            flops=flops, bytes_accessed=6 * tok_rows * features + 8 * BLK * features,
            transcendentals=0,
        ),
    )(expert_ids.T, tokens, out_grads)
    shape = (ROWS_DEV, EXP_DEV, features)
    return act.reshape(shape), grad.reshape(shape)


def solution(mesh):
    placed = (
        P(("groups", "dp", "expert"), None),
        P(("groups", "dp", "expert"), None, None),
        P(("groups", "dp", "expert"), None),
    )
    return jax.shard_map(
        functools.partial(on_device, mesh.shape["dp"]),
        mesh=mesh,
        in_specs=placed,
        out_specs=(P(("groups", "dp"), "expert", None), P(("groups", "dp"), "expert", None)),
        check_vma=False,
    )
```

time: 202 us -> 39.7 us (0.20)
  waiting for transfers between devices: 131 us -> 0 us
  Pallas kernels: 0 us -> 35.5 us
  local copies, waits for them, and re-layouts: 35.8 us -> 3.45 us
  between operations: 14.8 us -> 0.64 us
  starting transfers between devices: 12.1 us -> 0 us
  matrix products: 4.41 us -> 0 us
  other arithmetic: 3.24 us -> 0 us
    unnamed x2 -> x0, waiting for transfers between devices: 131 us -> none
    pallas_call x0 -> x1, Pallas kernels: none -> 35.5 us  [on_device(): pl.pallas_call(functools.partial(kernel, n, width, total), out_shape=(out...]
    scatter x2 -> x0, local copies, waits for them, and re-layouts: 17.9 us -> none  [build_buffer(): return empty.at[target].set(rows)]
    all_to_all x2 -> x0, starting transfers between devices: 12 us -> none  [the longest x1 6.21 us: on_device(): lax.all_to_all(input_send, 'expert', split_axis=0, concat_axis=1, tiled=T...]
    all_to_all x2 -> x0, local copies, waits for them, and re-layouts: 5.28 us -> none  [the longest x1 2.64 us: on_device(): lax.all_to_all(input_send, 'expert', split_axis=0, concat_axis=1, tiled=T...]
    dot_general x2 -> x0, matrix products: 4.41 us -> none  [the longest x1 2.21 us: on_device(): jnp.einsum('nsr,nsc->rnc', grad_recv[:, :, :slab_rows], grad_recv, prefer...]
    broadcast_in_dim x1 -> x0, local copies, waits for them, and re-layouts: 3.3 us -> none  [on_device(): jnp.broadcast_to(tokens[:, None, :], (tok_rows, top_count, features))]
    unnamed x8 -> x0, local copies, waits for them, and re-layouts: 3.04 us -> none
  transfers between devices with their start and end apart: 3 -> 0, of which waited for: 1 -> 0; matrix products, arithmetic and copies ran while one was open for 8% -> 0% of each run, Pallas kernels for 0% -> 0%
where the time goes in v1:
time: 39.7 us; the launch traced here: 39.5 us
  Pallas kernels  35.5 us (89%)
  local copies, waits for them, and re-layouts  3.45 us (9%)
  between operations  0.64 us (2%)
    pallas_call x1, Pallas kernels, on_device(): pl.pallas_call(functools.partial(kernel, n, width, total), out_shape=(out...  35.5 us
    reshape x2, local copies, waits for them, and re-layouts, on_device(): return (act.reshape(shape), grad.reshape(shape))  3.45 us

profile of v1, /device:TPU:0, one launch (start us, length us, event | category | flops | bytes accessed | tf_op | source)
XLA Modules:
  0.0 39.5 jit_solution(13906292954349384865)
XLA Ops:
  0.6 35.5 %shard_map.50 = (f32[8,6144]{1,0:T(8,128)}, f32[8,6144]{1,0:T(8,128)}) custom-call(s32[2,128]{1,0:T(2,128)} %bitcast.1, bf16[128,6144]{1,0:T(8,128)(2,1)} %tok_ref.1, bf16[128,2,6144]{2,1,0:T(2,128)(2,1)} %grad_ref.1), custom_call_target="tpu_custom_call" | custom-call | flops 603979776 | bytes 5111808 | tf_op jit(solution)/shard_map/pallas_call | solution.py:232
  36.1 1.7 %reshape.10 = f32[4,2,6144]{2,1,0:T(2,128)} reshape(f32[8,6144]{1,0:T(8,128)} %get-tuple-element.4) | data formatting | bytes 393216 | tf_op jit(solution)/shard_map/reshape | solution.py:263
  37.8 1.7 %reshape.11 = f32[4,2,6144]{2,1,0:T(2,128)} reshape(f32[8,6144]{1,0:T(8,128)} %get-tuple-element.5) | data formatting | bytes 393216 | tf_op jit(solution)/shard_map/reshape | solution.py:263

commit v2 on v1

v2 whole, which is shorter than its diff:
```python
import functools

import jax
import jax.numpy as jnp
from jax import lax
from jax.experimental import pallas as pl
from jax.experimental.pallas import tpu as pltpu
from jax.sharding import PartitionSpec as P

EXP_DEV = 2
ROWS_DEV = 4
BLK = EXP_DEV * ROWS_DEV
PAIR = 2 * BLK
LANES = 128
WIDTHS = (512, 1024, 1024, 1024, 1024, 1024, 512)
STEPS = 8.0
FULL = 32760.0
TINY = 1e-37
LAG_Y, LAG_Z, LAG_OUT = 1, 3, 4


def step_of(top):
    return jnp.ceil(jnp.log2(jnp.maximum(top, TINY)) * STEPS)


def scale_of(step):
    return jnp.exp2(step * (-1.0 / STEPS)) * FULL


def narrow(x):
    return jnp.round(x).astype(jnp.int32).astype(jnp.int16)


def widen(x):
    return x.astype(jnp.int32).astype(jnp.float32)


def unit_of(codes):
    return jnp.exp2(widen(codes) * (1.0 / STEPS)) * (1.0 / FULL)


def top_of(tiles):
    return functools.reduce(jnp.maximum, [jnp.abs(t) for t in tiles])


def widths_of(features):
    return WIDTHS if sum(WIDTHS) == features else (LANES,) * (features // LANES)


def starts_of(sizes):
    return [sum(sizes[:i]) for i in range(len(sizes))]


def kernel(
    n, total,
    ids_ref, tok_ref, grad_ref, act_ref, gout_ref,
    x_buf, g_buf, part, r0, s1, r1, s2, r2,
    in_sem, s0_sem, r0_sem, s1_sem, r1_sem, s2_sem, r2_sem,
):
    tok_rows, features = tok_ref.shape
    widths = widths_of(features)
    items = len(widths)
    begin = starts_of(widths)
    tiles = [w // LANES for w in widths]
    nz = n // 2
    half = n * PAIR
    quarter = half // 2
    blocks = quarter // PAIR
    marks = -(-2 * blocks // PAIR)
    y_tiles = [blocks * t + marks for t in tiles]
    y_at = starts_of(y_tiles)
    z_tiles = [t + 1 for t in tiles]
    z_at = starts_of(z_tiles)
    cols = [pl.ds(b, w) for b, w in zip(begin, widths)]
    core = lax.axis_index("expert")
    d = lax.axis_index("dp")
    z, y = d // 2, lax.rem(d, 2)

    flat = grad_ref.reshape(2 * tok_rows, features)
    loads = []
    for i in range(items):
        at = (slice(None), cols[i])
        pair = (
            pltpu.make_async_copy(tok_ref.at[at], x_buf.at[at], in_sem.at[0, i]),
            pltpu.make_async_copy(flat.at[at], g_buf.at[at], in_sem.at[1, i]),
        )
        loads.append(pair)
    for c in loads[0]:
        c.start()

    sibling = {"expert": 1 - core}
    across = {"dp": z * 2 + 1 - y}
    peers = [{"dp": lax.rem(z + 1 + j, nz) * 2 + y} for j in range(nz - 1)]
    barrier = pltpu.get_barrier_semaphore()
    for dev in [sibling, across] + peers:
        pl.semaphore_signal(barrier, inc=1, device_id=dev, device_id_type=pl.DeviceIdType.MESH)

    m_rows = 2 * n * BLK
    slab = -(-ROWS_DEV * n // LANES) * LANES

    def row_of(m):
        zd = z + 1 + (m & (n * BLK // 2 - 1)) // BLK
        zd = jnp.where(zd >= nz, zd - nz, zd)
        yd = (y + 1 + (m & (n * BLK - 1)) // (n * BLK // 2)) & 1
        return ROWS_DEV * (2 * zd + yd) + (m & (BLK - 1)) // EXP_DEV

    def expert_of(m):
        return EXP_DEV * ((core + 1 + m // (n * BLK)) & 1) + (m & (EXP_DEV - 1))

    pick = (
        row_of(lax.broadcasted_iota(jnp.int32, (m_rows, slab), 0))
        == lax.broadcasted_iota(jnp.int32, (m_rows, slab), 1)
    ).astype(jnp.float32).astype(jnp.bfloat16)
    ids = ids_ref[...]
    spread = (
        lax.broadcasted_iota(jnp.int32, (tok_rows, 2 * tok_rows), 1) // 2
        == lax.broadcasted_iota(jnp.int32, (tok_rows, 2 * tok_rows), 0)
    ).astype(jnp.float32).astype(jnp.bfloat16)
    ids_f = ids.astype(jnp.float32)
    both = jnp.dot(ids_f.astype(jnp.bfloat16), spread, preferred_element_type=jnp.float32)
    odd = (lax.broadcasted_iota(jnp.int32, (1, 2 * tok_rows), 1) & 1) == 1
    ids_flat = jnp.where(odd, both[1:2, :], both[0:1, :])
    e_tok = expert_of(lax.broadcasted_iota(jnp.int32, (m_rows, tok_rows), 0)).astype(jnp.float32)
    e_pair = expert_of(lax.broadcasted_iota(jnp.int32, (m_rows, 2 * tok_rows), 0)).astype(
        jnp.float32
    )
    nt = (((1,), (1,)), ((), ()))

    for c in loads[0]:
        c.wait()
    for pair in loads[1:]:
        for c in pair:
            c.start()
    left_x = lax.dot_general(pick, x_buf[:, :slab], nt, preferred_element_type=jnp.float32)
    left_g = lax.dot_general(pick, g_buf[:, :slab], nt, preferred_element_type=jnp.float32)
    hit_x = (e_tok == ids_f[0:1, :]) | (e_tok == ids_f[1:2, :])
    left_x = jnp.where(hit_x, left_x, 0.0).astype(jnp.bfloat16)
    left_g = jnp.where(e_pair == ids_flat, left_g, 0.0).astype(jnp.bfloat16)

    def send(src, dst, s_sem, r_sem, dev):
        return pltpu.make_async_remote_copy(
            src_ref=src, dst_ref=dst, send_sem=s_sem, recv_sem=r_sem,
            device_id=dev, device_id_type=pl.DeviceIdType.MESH,
        )

    core_copy = [
        send(
            part.at[pl.ds(0, half), cols[i]], r0.at[:, cols[i]],
            s0_sem.at[i], r0_sem.at[i], sibling,
        )
        for i in range(items)
    ]
    y_copy = []
    z_copy = []
    for i in range(items):
        run = pl.ds(y_at[i], y_tiles[i])
        y_copy.append(send(s1.at[run], r1.at[run], s1_sem.at[i], r1_sem.at[i], across))
        run = pl.ds(z_at[i], z_tiles[i])
        z_copy.append([
            send(
                s2.at[j, run], r2.at[j, run], s2_sem.at[i, j], r2_sem.at[i, j], peers[j]
            )
            for j in range(nz - 1)
        ])

    def local_terms(i):
        for a, (left, buf) in enumerate(((left_x, x_buf), (left_g, g_buf))):
            term = jnp.dot(left, buf[:, cols[i]], preferred_element_type=jnp.float32)
            for b in range(m_rows // BLK):
                part[b * PAIR + a * BLK : b * PAIR + (a + 1) * BLK, cols[i]] = term[
                    b * BLK : (b + 1) * BLK
                ]

    def lane(i, j):
        return slice(begin[i] + j * LANES, begin[i] + (j + 1) * LANES)

    def chip_terms(i):
        core_copy[i].wait_recv()
        steps = []
        for b in range(blocks):
            rows = slice(b * PAIR, (b + 1) * PAIR)
            own = slice(half + b * PAIR, half + (b + 1) * PAIR)
            sums = [part[own, lane(i, j)] + r0[rows, lane(i, j)] for j in range(tiles[i])]
            top = top_of(sums)
            scales = []
            for h in range(2):
                step = step_of(jnp.max(top[h * BLK : (h + 1) * BLK], axis=0, keepdims=True))
                steps.append(step)
                scales.append(jnp.broadcast_to(scale_of(step), (BLK, LANES)))
            scale = jnp.concatenate(scales, axis=0)
            for j, v in enumerate(sums):
                s1[y_at[i] + b * tiles[i] + j] = narrow(v * scale)
        steps += [jnp.zeros((1, LANES), jnp.float32)] * (marks * PAIR - len(steps))
        for m in range(marks):
            mark = jnp.concatenate(steps[m * PAIR : (m + 1) * PAIR], axis=0)
            s1[y_at[i] + blocks * tiles[i] + m] = narrow(mark)
        y_copy[i].start()

    def pair_terms(i):
        y_copy[i].wait_recv()
        units = [unit_of(r1[y_at[i] + blocks * tiles[i] + m]) for m in range(marks)]
        for b in range(blocks):
            near = slice(quarter + b * PAIR, quarter + (b + 1) * PAIR)
            own = slice(half + quarter + b * PAIR, half + quarter + (b + 1) * PAIR)
            unit = jnp.concatenate(
                [
                    jnp.broadcast_to(units[k // PAIR][k % PAIR : k % PAIR + 1], (BLK, LANES))
                    for k in (2 * b, 2 * b + 1)
                ],
                axis=0,
            )
            sums = [
                part[own, lane(i, j)]
                + r0[near, lane(i, j)]
                + widen(r1[y_at[i] + b * tiles[i] + j]) * unit
                for j in range(tiles[i])
            ]
            if b < blocks - 1:
                step = step_of(top_of(sums))
                scale = scale_of(step)
                for j, v in enumerate(sums):
                    s2[b, z_at[i] + j] = narrow(v * scale)
                s2[b, z_at[i] + tiles[i]] = narrow(step)
                z_copy[i][b].start()
            else:
                for j in range(tiles[i]):
                    part[own, lane(i, j)] = sums[j]

    def outputs(i):
        for c in z_copy[i]:
            c.wait_recv()
        last = slice(2 * half - PAIR, 2 * half)
        units = [unit_of(r2[b, z_at[i] + tiles[i]]) for b in range(nz - 1)]
        for j in range(tiles[i]):
            acc = part[last, lane(i, j)]
            for b in range(nz - 1):
                acc = acc + widen(r2[b, z_at[i] + j]) * units[b]
            acc = acc * (1.0 / total)
            act_ref[:, :, lane(i, j)] = acc[:BLK].reshape(ROWS_DEV, EXP_DEV, LANES)
            gout_ref[:, :, lane(i, j)] = acc[BLK:].reshape(ROWS_DEV, EXP_DEV, LANES)

    for t in range(items + LAG_OUT):
        if t < items:
            if t:
                for c in loads[t]:
                    c.wait()
            local_terms(t)
            if t == 0:
                pl.semaphore_wait(barrier, nz + 1)
            core_copy[t].start()
        if 0 <= t - LAG_Y < items:
            chip_terms(t - LAG_Y)
        if 0 <= t - LAG_Z < items:
            pair_terms(t - LAG_Z)
        if 0 <= t - LAG_OUT < items:
            outputs(t - LAG_OUT)

    for i in range(items):
        core_copy[i].wait_send()
        y_copy[i].wait_send()
        for c in z_copy[i]:
            c.wait_send()


def hand_over(act_ref, grad_ref, act_out, grad_out):
    act_out[...] = act_ref[...]
    grad_out[...] = grad_ref[...]


def on_device(n, tokens, out_grads, expert_ids):
    tok_rows, features = tokens.shape
    widths = widths_of(features)
    items = len(widths)
    nz = n // 2
    half = n * PAIR
    blocks = half // 2 // PAIR
    marks = -(-2 * blocks // PAIR)
    tiles = features // LANES
    y_shape = (blocks * tiles + marks * items, PAIR, LANES)
    z_shape = (nz - 1, tiles + items, PAIR, LANES)
    total = tok_rows * n * 2
    vmem = pl.BlockSpec(memory_space=pltpu.VMEM)
    hbm = pl.BlockSpec(memory_space=pl.ANY)
    out = jax.ShapeDtypeStruct((ROWS_DEV, EXP_DEV, features), jnp.float32)
    dma = pltpu.SemaphoreType.DMA
    flops = 2 * 3 * tok_rows * 2 * n * BLK * features
    act, grad = pl.pallas_call(
        functools.partial(kernel, n, total),
        out_shape=(out, out),
        in_specs=[vmem, hbm, hbm],
        out_specs=(vmem, vmem),
        scratch_shapes=[
            pltpu.VMEM((tok_rows, features), jnp.bfloat16),
            pltpu.VMEM((2 * tok_rows, features), jnp.bfloat16),
            pltpu.VMEM((2 * half, features), jnp.float32),
            pltpu.VMEM((half, features), jnp.float32),
            pltpu.VMEM(y_shape, jnp.int16),
            pltpu.VMEM(y_shape, jnp.int16),
            pltpu.VMEM(z_shape, jnp.int16),
            pltpu.VMEM(z_shape, jnp.int16),
            dma((2, items)),
            dma((items,)),
            dma((items,)),
            dma((items,)),
            dma((items,)),
            dma((items, nz - 1)),
            dma((items, nz - 1)),
        ],
        compiler_params=pltpu.CompilerParams(
            collective_id=0, has_side_effects=True, vmem_limit_bytes=61 * 1024 * 1024
        ),
        cost_estimate=pl.CostEstimate(
            flops=flops, bytes_accessed=6 * tok_rows * features + 8 * BLK * features,
            transcendentals=0,
        ),
    )(expert_ids.T, tokens, out_grads)
    return pl.pallas_call(
        hand_over,
        out_shape=(out, out),
        in_specs=[vmem, vmem],
        out_specs=(vmem, vmem),
    )(act, grad)


def solution(mesh):
    placed = (
        P(("groups", "dp", "expert"), None),
        P(("groups", "dp", "expert"), None, None),
        P(("groups", "dp", "expert"), None),
    )
    return jax.shard_map(
        functools.partial(on_device, mesh.shape["dp"]),
        mesh=mesh,
        in_specs=placed,
        out_specs=(P(("groups", "dp"), "expert", None), P(("groups", "dp"), "expert", None)),
        check_vma=False,
    )
```

time: 39.7 us -> 37.1 us (0.935)
  local copies, waits for them, and re-layouts: 3.45 us -> 0 us
  Pallas kernels: 35.5 us -> 36.3 us
    reshape x2 -> x0, local copies, waits for them, and re-layouts: 3.45 us -> none  [on_device(): return (act.reshape(shape), grad.reshape(shape))]
    pallas_call x1 -> x2, Pallas kernels: 35.5 us -> 36.3 us  [the longest x1 34.5 us: on_device(): pl.pallas_call(functools.partial(kernel, n, total), out_shape=(out, out),...]
where the time goes in v2:
time: 37.1 us; the launch traced here: 36.9 us
  Pallas kernels  36.3 us (98%)
  between operations  0.64 us (2%)
    pallas_call x1, Pallas kernels, on_device(): pl.pallas_call(functools.partial(kernel, n, total), out_shape=(out, out),...  34.5 us
    pallas_call x1, Pallas kernels, on_device(): pl.pallas_call(hand_over, out_shape=(out, out), in_specs=[vmem, vmem], ou...  1.78 us

profile of v2, /device:TPU:0, one launch (start us, length us, event | category | flops | bytes accessed | tf_op | source)
XLA Modules:
  0.0 36.9 jit_solution(8925694999788287835)
XLA Ops:
  0.6 34.5 %shard_map.50 = (f32[4,2,6144]{2,1,0:T(2,128)}, f32[4,2,6144]{2,1,0:T(2,128)}) custom-call(s32[2,128]{1,0:T(2,128)} %bitcast.1, bf16[128,6144]{1,0:T(8,128)(2,1)} %tok_ref.1, bf16[128,2,6144]{2,1,0:T(2,128)(2,1)} %grad_ref.1), custom_call_target="tpu_custom_call" | custom-call | flops 603979776 | bytes 5111808 | tf_op jit(solution)/shard_map/pallas_call | solution.py:287
  35.2 1.8 %shard_map.51 = (f32[4,2,6144]{2,1,0:T(2,128)}, f32[4,2,6144]{2,1,0:T(2,128)}) custom-call(f32[4,2,6144]{2,1,0:T(2,128)} %get-tuple-element.4.act_ref, f32[4,2,6144]{2,1,0:T(2,128)} %get-tuple-element.5.grad_ref), custom_call_target="tpu_custom_call" | custom-call | tf_op jit(solution)/shard_map/pallas_call | solution.py:317

commit v3 on v2

--- a/solution.py
+++ b/solution.py
@@ -12,11 +12,11 @@
 BLK = EXP_DEV * ROWS_DEV
 PAIR = 2 * BLK
 LANES = 128
-WIDTHS = (512, 1024, 1024, 1024, 1024, 1024, 512)
+WIDTHS = (1024, 1024, 1024, 1024, 1024, 1024)
 STEPS = 8.0
 FULL = 32760.0
 TINY = 1e-37
-LAG_Y, LAG_Z, LAG_OUT = 1, 3, 4
+LAG_Y, LAG_Z, LAG_OUT = 1, 2, 4
 
 
 def step_of(top):

time: 37.1 us -> 37.1 us (level)
  no operation moved by 1% of the time
where the time goes in v3:
time: 37.1 us; the launch traced here: 37 us
  Pallas kernels  36.3 us (98%)
  between operations  0.64 us (2%)
    pallas_call x1, Pallas kernels, on_device(): pl.pallas_call(functools.partial(kernel, n, total), out_shape=(out, out),...  34.5 us
    pallas_call x1, Pallas kernels, on_device(): pl.pallas_call(hand_over, out_shape=(out, out), in_specs=[vmem, vmem], ou...  1.78 us

profile of v3, /device:TPU:0, one launch (start us, length us, event | category | flops | bytes accessed | tf_op | source)
XLA Modules:
  0.0 37.0 jit_solution(3247039817291655248)
XLA Ops:
  0.6 34.5 %shard_map.50 = (f32[4,2,6144]{2,1,0:T(2,128)}, f32[4,2,6144]{2,1,0:T(2,128)}) custom-call(s32[2,128]{1,0:T(2,128)} %bitcast.1, bf16[128,6144]{1,0:T(8,128)(2,1)} %tok_ref.1, bf16[128,2,6144]{2,1,0:T(2,128)(2,1)} %grad_ref.1), custom_call_target="tpu_custom_call" | custom-call | flops 603979776 | bytes 5111808 | tf_op jit(solution)/shard_map/pallas_call | solution.py:287
  35.2 1.8 %shard_map.51 = (f32[4,2,6144]{2,1,0:T(2,128)}, f32[4,2,6144]{2,1,0:T(2,128)}) custom-call(f32[4,2,6144]{2,1,0:T(2,128)} %get-tuple-element.4.act_ref, f32[4,2,6144]{2,1,0:T(2,128)} %get-tuple-element.5.grad_ref), custom_call_target="tpu_custom_call" | custom-call | tf_op jit(solution)/shard_map/pallas_call | solution.py:317
